TPU v7x, 32 devices: a whole 2x2x4 slice. The times are simulated.
32 devices in a mesh: dp: 4 (over z), seq: 8 (over y, x, core).
Axes of the slice: x: 2, y: 2, z: 4, core: 2. Of those that a mesh axis runs over, the one named last changes fastest.
Arguments:
- inputs: bfloat16 [4, 2048, 5120], P('dp', 'seq'), may hold values from -6 to 6
- gate_proj: bfloat16 [4, 2048, 5120], P('dp', 'seq'), may hold values from -6 to 6
- write_proj: bfloat16 [4, 2048, 128], P('dp', 'seq'), may hold values from -6 to 6
- read_proj: bfloat16 [4, 2048, 128], P('dp', 'seq'), may hold values from -6 to 6
- step_size: float32 [4, 80, 2048], P('dp', None, 'seq'), may hold values from 0 to 0.4, as said below
- log_forget: float32 [4, 80, 2048], P('dp', None, 'seq'), may hold values from -0.8 to 0, as said below
- conv_weight: float32 [4, 5376], replicated, may hold values from -3 to 3
- conv_bias: float32 [5376], replicated, may hold values from -3 to 3
- skip_gain: float32 [80], replicated, may hold values from 0.5 to 1.5
- norm_gain: float32 [5120], replicated, may hold values from 0.1 to 1.9
- code_weight: bfloat16 [5120, 256], P('dp'), may hold values from -0.5 to 0.5
- prior_draw: float32 [256, 256], P(('dp', 'seq')), may hold values from -6 to 6
Outputs:
- mixed: bfloat16 [4, 2048, 5120], P('dp', 'seq')
- codes: float32 [256, 256], P(('dp', 'seq'))
- kernel: float32 [256, 512], P(('dp', 'seq'))
Inputs may be any that keep to these rules, and one draw needn't show every extreme that they name: `step_size`: positive step sizes, per document, head and position. `log_forget`: never positive.
All inputs are finite; a program needn't handle non-finite values.
Results may differ from a plain program's by a relative error of at most 0.008.
Values may be sent and summed in bfloat16 or wider, within the bound.
A program may use at most 256 MiB of HBM per device.

v0:
```python
import jax
import jax.numpy as jnp
from jax import lax
from jax.sharding import PartitionSpec as P

SPAN = 128
SEG = 32


def passed_along(block, axis, distance):
    devices = range(lax.axis_size(axis))
    route = [(i - distance, i) for i in devices if i - distance in devices]
    return lax.ppermute(block, axis, route)


def carried_in(part, axis, combine, identity):
    place = lax.axis_index(axis)
    gathered = jax.tree.map(lambda a: lax.all_gather(a, axis), part)
    state = jax.tree.map(lambda a, e: jnp.zeros_like(a) + jnp.asarray(e, a.dtype), part, identity)

    def one(step, state):
        return combine(
            state, jax.tree.map(lambda a: lax.dynamic_index_in_dim(a, step, 0, False), gathered)
        )

    return lax.fori_loop(0, place, one, state)


def block_terms(values, write_rows, read_rows, steps, logs):
    cum_log = jnp.cumsum(logs, axis=1)
    length = logs.shape[1]
    causal = jnp.arange(length)[:, None] >= jnp.arange(length)[None, :]
    scores = jnp.dot(read_rows, write_rows.T, preferred_element_type=jnp.float32)
    decay = jnp.exp(jnp.where(causal[None], cum_log[:, :, None] - cum_log[:, None, :], -jnp.inf))
    mixing = (scores[None] * decay * steps[:, None, :]).astype(jnp.bfloat16)
    inner_out = jnp.einsum("hts,shp->thp", mixing, values, preferred_element_type=jnp.float32)
    tail_decay = jnp.exp(cum_log[:, -1:] - cum_log) * steps
    weighted = (tail_decay[:, :, None] * write_rows.astype(jnp.float32)[None]).astype(jnp.bfloat16)
    states = jnp.einsum("hsn,shp->hpn", weighted, values, preferred_element_type=jnp.float32)
    return (inner_out, states, cum_log)


def join_states(first, second):
    return (first[0] + second[0], jnp.exp(second[0])[:, None, None] * first[1] + second[1])


def per_device(
    inputs,
    gate_proj,
    write_proj,
    read_proj,
    step_size,
    log_forget,
    conv_weight,
    conv_bias,
    skip_gain,
    norm_gain,
    code_weight,
    prior_draw,
):
    length = inputs.shape[1]
    width = inputs.shape[2]
    state_dim = write_proj.shape[2]
    heads = step_size.shape[1]
    head_dim = width // heads
    taps = conv_weight.shape[0]
    joined = jnp.concatenate([inputs[0], write_proj[0], read_proj[0]], axis=1)
    rim_rows = passed_along(joined[length - (taps - 1) :], "seq", 1)
    padded = jnp.concatenate([rim_rows, joined], axis=0)
    summed = conv_bias[None, :] + conv_weight[0][None, :] * padded[0:length].astype(jnp.float32)
    for offset in range(1, taps):
        summed = summed + conv_weight[offset][None, :] * padded[offset : offset + length].astype(
            jnp.float32
        )
    active = jax.nn.silu(summed).astype(jnp.bfloat16)
    values = active[:, :width].reshape(length, heads, head_dim)
    write_all = active[:, width : width + state_dim]
    read_all = active[:, width + state_dim :]
    steps = step_size[0]
    logs = log_forget[0]
    blocks = length // SPAN
    inner_list = []
    state_list = []
    cum_list = []
    for block in range(blocks):
        lower = block * SPAN
        upper = lower + SPAN
        inner_out, states, cum_log = block_terms(
            values[lower:upper],
            write_all[lower:upper],
            read_all[lower:upper],
            steps[:, lower:upper],
            logs[:, lower:upper],
        )
        inner_list.append(inner_out)
        state_list.append(states)
        cum_list.append(cum_log)
    running = jnp.zeros((heads, head_dim, state_dim), jnp.float32)
    before = jnp.zeros((heads,), jnp.float32)
    start_list = []
    before_list = []
    for block in range(blocks):
        start_list.append(running)
        before_list.append(before)
        block_total = cum_list[block][:, -1]
        running = jnp.exp(block_total)[:, None, None] * running + state_list[block]
        before = before + block_total
    identity = (jnp.zeros_like(before), jnp.zeros_like(running))
    decay_in, carry_in = carried_in((before, running), "seq", join_states, identity)
    outputs = []
    for block in range(blocks):
        lower = block * SPAN
        upper = lower + SPAN
        start = start_list[block] + jnp.exp(before_list[block])[:, None, None] * carry_in
        read_block = read_all[lower:upper].astype(jnp.float32)
        outer_out = jnp.exp(cum_list[block]).T[:, :, None] * jnp.einsum(
            "tn,hpn->thp", read_block, start, precision=lax.Precision.HIGHEST
        )
        outputs.append(inner_list[block] + outer_out)
    ssd_out = jnp.concatenate(outputs, axis=0)
    total = ssd_out + skip_gain[None, :, None] * values.astype(jnp.float32)
    gated = total.reshape(length, width) * jax.nn.silu(gate_proj[0].astype(jnp.float32))
    scale = lax.rsqrt(jnp.mean(gated * gated, axis=1, keepdims=True) + 1e-05)
    mixed = (gated * scale * norm_gain[None, :]).astype(jnp.bfloat16)
    pooled = jnp.mean(mixed.astype(jnp.float32).reshape(length // SEG, SEG, width), axis=1).astype(
        jnp.bfloat16
    )
    codes_local = jnp.dot(
        pooled,
        lax.all_gather(code_weight, "dp", axis=0, tiled=True),
        preferred_element_type=jnp.float32,
    )
    all_codes, all_prior = (
        lax.all_gather(codes_local, ("dp", "seq"), axis=0, tiled=True),
        lax.all_gather(prior_draw, ("dp", "seq"), axis=0, tiled=True),
    )
    columns = jnp.concatenate([all_codes, all_prior], axis=0)
    cross = jnp.dot(codes_local, columns.T, precision=lax.Precision.HIGHEST)
    row_sq = jnp.sum(codes_local * codes_local, axis=1)
    col_sq = jnp.sum(columns * columns, axis=1)
    dist_sq = row_sq[:, None] + col_sq[None, :] - 2.0 * cross
    code_dim = codes_local.shape[1]
    kernel = 2.0 * code_dim / (2.0 * code_dim + dist_sq)
    return (mixed[None], codes_local, kernel)


def solution(mesh):
    in_specs = (
        P("dp", "seq", None),
        P("dp", "seq", None),
        P("dp", "seq", None),
        P("dp", "seq", None),
        P("dp", None, "seq"),
        P("dp", None, "seq"),
        P(),
        P(),
        P(),
        P(),
        P("dp", None),
        P(("dp", "seq"), None),
    )
    out_specs = (P("dp", "seq", None), P(("dp", "seq"), None), P(("dp", "seq"), None))
    return jax.shard_map(
        per_device, mesh=mesh, in_specs=in_specs, out_specs=out_specs, check_vma=False
    )
```

profile of v0, /device:TPU:0, one launch (start us, length us, event | category | flops | bytes accessed | tf_op | source)
XLA Modules:
  0.0 257.2 jit_solution(8779283257993149591)
XLA Ops:
  7.2 0.0 all-gather.7.cloned.1.call-start
  7.2 0.0 copy-start.2
  7.3 2.1 pad_maximum_fusion
  9.5 2.4 collective-permute-start
  11.8 0.3 reduce_window_sum.17
  12.1 0.3 reduce_window_sum.18
  12.4 0.2 slice_reduce_fusion
  12.7 0.1 fusion.53
  12.8 0.2 slice_reduce_fusion.5
  13.0 0.0 copy-start.3
  13.1 0.0 copy-start.14
  13.1 2.4 maximum_maximum_fusion
  15.5 4.4 %multiply_convert_fusion = bf16[256,5376]{1,0:T(8,128)(2,1)S(1)} fusion(bf16[259,5376]{1,0:T(8,128)(2,1)S(1)} %maximum_maximum_fusion, f32[5376]{0:T(1024)S(1)} %get-tuple-element.50, f32[5376]{0:T(1024)S(1)} %get-tuple-element.51, f32[5376]{0:T(1024)S(1)} %get-tuple-element.49, f32[5376]{0:T(1024)S(1)} %get-tuple-element.48, f32[5376]{0:T(1024)S(1)} %copy-done.14, ...), kind=kLoop, calls=%fused_computation.4 | loop fusion | flops 30277632 | bytes 13870080 | tf_op jit(solution)/shard_map/convert_element_type | solution.py:75
  19.9 2.0 fusion.52
  21.9 2.4 copy.31
  24.4 2.4 copy.32
  26.8 3.9 %fusion.6 = f32[80,64,128]{2,1,0:T(8,128)S(1)} fusion(bf16[128,80,64]{0,2,1:T(8,128)(2,1)} %bitcast.56, f32[128,128]{1,0:T(8,128)S(1)} %get-tuple-element.68, f32[80,128]{1,0:T(8,128)S(1)} %get-tuple-element.72), kind=kOutput, calls=%fused_computation.21 | convolution fusion | flops 170393600 | bytes 4038656 | tf_op jit(solution)/shard_map/hsn,shp->hpn/dot_general | solution.py:39
  30.7 1.5 copy-done.4
  32.2 4.0 %multiply_add_fusion = f32[80,64,128]{2,1,0:T(8,128)} fusion(f32[80,64,128]{2,1,0:T(8,128)S(1)} %fusion.6, bf16[128,80,64]{0,2,1:T(8,128)(2,1)S(1)} %bitcast.58, f32[128,128]{1,0:T(8,128)S(1)} %get-tuple-element.67, f32[80,128]{1,0:T(8,128)S(1)} %get-tuple-element.73, f32[80]{0:T(128)S(1)} %get-tuple-element.80, f32[80]{0:T(128)S(1)} %exp.64), kind=kOutput, calls=%fused_computation.34 | convolution fusion | flops 172359680 | bytes 6660736 | tf_op jit(solution)/shard_map/hsn,shp->hpn/dot_general | solution.py:39
  36.2 0.0 all-gather.7.cloned.1.call-update
  36.2 0.0 all-gather.5.cloned.1.call-start
  36.3 0.7 all-gather.5.cloned.1.call-update
  37.0 0.6 dynamic-slice
  38.3 0.2 dynamic-update-slice
  38.5 14.7 %all-reduce = f32[640]{0:T(1024)S(1)} all-reduce(f32[640]{0:T(1024)S(1)} %dynamic-update-slice), channel_id=2, replica_groups=mesh['dp'=4,'seq'=8] {'seq'}, use_global_device_ids=true, to_apply=%add | all-reduce | flops 640 | bytes 5120
  53.2 0.1 reshape.99
  53.3 0.1 mul.251
  53.4 0.1 mul.252
  53.5 41.6 %all_gather.24 = f32[256,256]{1,0:T(8,128)S(1)} all-gather(f32[8,256]{1,0:T(8,128)S(1)} %copy-done.15), channel_id=1, replica_groups=mesh['dp'=4,'seq'=8] {'dp','seq'}, dimensions={0}, use_global_device_ids=true | all-gather | bytes 270336 | tf_op jit(solution)/shard_map/all_gather | solution.py:135
  95.1 0.1 fusion.43
  95.3 0.1 fusion.40
  95.4 4.5 %fusion.4 = f32[80,64,128]{2,1,0:T(8,128)} fusion(bf16[128,80,64]{0,2,1:T(8,128)(2,1)} %bitcast.57, f32[80,128]{1,0:T(8,128)S(1)} %get-tuple-element.71, f32[80,128]{1,0:T(8,128)S(1)} %reduce_window_sum.17, f32[128,128]{1,0:T(8,128)S(1)} %fusion.43, pred[128,128]{1,0:T(8,128)(4,1)S(1)} %iota_compare_fusion), kind=kOutput, calls=%fused_computation.19 | convolution fusion | flops 174325760 | bytes 4096000 | tf_op jit(solution)/shard_map/hts,shp->thp/dot_general | solution.py:36
  99.9 4.0 %fusion.5 = f32[80,64,128]{2,1,0:T(8,128)} fusion(bf16[128,80,64]{0,2,1:T(8,128)(2,1)S(1)} %bitcast.59, f32[80,128]{1,0:T(8,128)S(1)} %get-tuple-element.74, f32[80,128]{1,0:T(8,128)S(1)} %reduce_window_sum.18, f32[128,128]{1,0:T(8,128)S(1)} %fusion.40, pred[128,128]{1,0:T(8,128)(4,1)S(1)} %iota_compare_fusion), kind=kOutput, calls=%fused_computation.20 | convolution fusion | flops 174325760 | bytes 4096000 | tf_op jit(solution)/shard_map/hts,shp->thp/dot_general | solution.py:36
  103.9 46.5 %all-gather.7.cloned.1.call-done = f32[640,64,128]{2,1,0:T(8,128)} async-done(((f32[80,64,128]{2,1,0:T(8,128)}), f32[640,64,128]{2,1,0:T(8,128)}) %all-gather.7.cloned.1.call-update) | async-done | bytes 20971536 | tf_op jit(solution)/shard_map/all_gather | solution.py:18
  150.4 0.3 broadcast.52
  150.8 0.2 while.12
  151.0 4.6 %bitcast_add_fusion.2 = f32[128,80,64]{0,2,1:T(8,128)} fusion(f32[80,64,128]{2,1,0:T(8,128)} %fusion.4, f32[80,64,128]{2,1,0:T(8,128)S(1)} %get-tuple-element.47, f32[128,80]{0,1:T(8,128)S(1)} %get-tuple-element.78, bf16[256,5376]{1,0:T(8,128)(2,1)} %copy-done), kind=kOutput, calls=%fused_computation.24 | convolution fusion | flops 1007943680 | bytes 7938048 | tf_op jit(solution)/shard_map/tn,hpn->thp/dot_general | solution.py:116
  155.6 3.2 %copy.37 = f32[128,5120]{1,0:T(8,128)} copy(f32[128,5120]{0,1:T(8,128)} %bitcast.53) | data formatting | bytes 5242880 | tf_op jit(solution)/shard_map/concatenate | solution.py:120
  158.8 6.0 %bitcast_add_fusion.1 = f32[128,80,64]{0,2,1:T(8,128)} fusion(f32[80,64,128]{2,1,0:T(8,128)} %fusion.5, f32[80,64,128]{2,1,0:T(8,128)S(1)} %get-tuple-element.47, f32[80,64,128]{2,1,0:T(8,128)} %copy-done.4, f32[80]{0:T(128)S(1)} %get-tuple-element.79, f32[128,80]{0,1:T(8,128)S(1)} %get-tuple-element.77, f32[80]{0:T(128)S(1)} %get-tuple-element.80, ...), kind=kOutput, calls=%fused_computation.23 | convolution fusion | flops 1009909760 | bytes 10560128 | tf_op jit(solution)/shard_map/tn,hpn->thp/dot_general | solution.py:116
  164.8 3.4 %copy.38 = f32[128,5120]{1,0:T(8,128)} copy(f32[128,5120]{0,1:T(8,128)} %bitcast.54) | data formatting | bytes 5242880 | tf_op jit(solution)/shard_map/concatenate | solution.py:120
  168.1 5.3 %multiply_reduce_fusion = (f32[256]{0:T(256)S(1)}, f32[256,5120]{1,0:T(8,128)S(1)}) fusion(bf16[1,256,5120]{2,1,0:T(8,128)(2,1)} %param.15, bf16[256,5376]{1,0:T(8,128)(2,1)S(1)} %copy-done.1, f32[5120]{0:T(1024)S(1)} %mul.252, f32[128,5120]{1,0:T(8,128)} %copy.38, f32[128,5120]{1,0:T(8,128)} %copy.37), kind=kLoop, calls=%fused_computation.12 | loop fusion | flops 15728384 | bytes 15750144 | tf_op jit(solution)/shard_map/reduce_sum | solution.py:123
  173.4 1.0 convert_reduce_fusion
  174.4 2.2 fusion.50
  176.6 30.2 %all-gather.5.cloned.1.call-done = bf16[5120,256]{1,0:T(8,128)(2,1)} async-done(((bf16[1280,256]{1,0:T(8,128)(2,1)}), bf16[5120,256]{1,0:T(8,128)(2,1)}) %all-gather.5.cloned.1.call-update) | async-done | bytes 2621456 | tf_op jit(solution)/shard_map/all_gather | solution.py:130
  206.8 2.3 multiply_reduce_fusion.2
  209.1 39.9 %all_gather.23 = f32[256,256]{1,0:T(8,128)S(1)} all-gather(f32[8,256]{1,0:T(8,128)S(1)} %get-tuple-element.82), channel_id=1, replica_groups=mesh['dp'=4,'seq'=8] {'dp','seq'}, dimensions={0}, use_global_device_ids=true | all-gather | bytes 270336 | tf_op jit(solution)/shard_map/all_gather | solution.py:134
  249.0 0.1 multiply_reduce_fusion.1
  249.2 1.1 fusion.34
  (43 shorter events, 0.2 us)
Async XLA Ops:
  7.2 143.3 %all-gather.7.cloned.1.call-start = ((), (), s32[]{:S(2)}) async-start(), calls=%async_computation.1 | async-start | bytes 23592960 | tf_op jit(solution)/shard_map/all_gather | solution.py:18
  7.2 4.6 %copy-start.11 = (f32[1,80,256]{2,1,0:T(8,128)S(1)}, f32[1,80,256]{2,1,0:T(8,128)}, u32[]{:S(2)}) copy-start(f32[1,80,256]{2,1,0:T(8,128)} %param.19) | copy-start | bytes 245764
  7.2 5.5 %copy-start.12 = (f32[1,80,256]{2,1,0:T(8,128)S(1)}, f32[1,80,256]{2,1,0:T(8,128)}, u32[]{:S(2)}) copy-start(f32[1,80,256]{2,1,0:T(8,128)} %param.18) | copy-start | bytes 245764
  7.2 5.6 %copy-start.9 = (f32[4,5376]{1,0:T(4,128)S(1)}, f32[4,5376]{1,0:T(4,128)}, u32[]{:S(2)}) copy-start(f32[4,5376]{1,0:T(4,128)} %param.20) | copy-start | bytes 258052
  7.2 5.8 %copy-start.2 = (bf16[1,256,5120]{2,1,0:T(8,128)(2,1)S(1)}, bf16[1,256,5120]{2,1,0:T(8,128)(2,1)}, u32[]{:S(2)}) copy-start(bf16[1,256,5120]{2,1,0:T(8,128)(2,1)} %param.14) | copy-start | bytes 7864324
  7.3 5.8 %copy-start.7 = (bf16[1,256,128]{2,1,0:T(8,128)(2,1)S(1)}, bf16[1,256,128]{2,1,0:T(8,128)(2,1)}, u32[]{:S(2)}) copy-start(bf16[1,256,128]{2,1,0:T(8,128)(2,1)} %param.17) | copy-start | bytes 196612
  7.3 5.8 %copy-start.8 = (bf16[1,256,128]{2,1,0:T(8,128)(2,1)S(1)}, bf16[1,256,128]{2,1,0:T(8,128)(2,1)}, u32[]{:S(2)}) copy-start(bf16[1,256,128]{2,1,0:T(8,128)(2,1)} %param.16) | copy-start | bytes 196612
  9.5 3.6 %collective-permute-start = (bf16[3,5376]{1,0:T(4,128)(2,1)S(1)}, bf16[3,5376]{1,0:T(4,128)(2,1)S(1)}, u32[]{:S(2)}, u32[]{:S(2)}) collective-permute-start(bf16[3,5376]{1,0:T(4,128)(2,1)S(1)} %slice.104), channel_id=1, source_target_pairs={{0,1},{1,2},{2,3},{3,4},{4,5},{5,6},{6,7},{8,9},{9,10},{10,11},{11... | collective-permute-start | bytes 96776 | tf_op jit(solution)/shard_map/ppermute | solution.py:13
  13.0 2.4 copy-start.3
  13.1 2.4 copy-start.14
  19.9 75.3 %copy-start = (bf16[256,5376]{1,0:T(8,128)(2,1)}, bf16[256,5376]{1,0:T(8,128)(2,1)S(1)}, u32[]{:S(2)}) copy-start(bf16[256,5376]{1,0:T(8,128)(2,1)S(1)} %multiply_convert_fusion) | copy-start | bytes 8257540
  26.8 5.4 %copy-start.5 = (bf16[128,5120]{0,1:T(8,128)(2,1)S(1)}, bf16[128,5120]{0,1:T(8,128)(2,1)}, u32[]{:S(2)}) copy-start(bf16[128,5120]{0,1:T(8,128)(2,1)} %copy.32) | copy-start | bytes 3932164
  30.7 1.5 copy-start.4
  36.2 0.8 copy-start.17
  36.2 17.1 %copy-start.16 = (f32[80]{0:T(128)S(1)}, f32[80]{0:T(128)}, u32[]{:S(2)}) copy-start(f32[80]{0:T(128)} %param.22) | copy-start | bytes 964
  36.2 17.3 %copy-start.15 = (f32[8,256]{1,0:T(8,128)S(1)}, f32[8,256]{1,0:T(8,128)}, u32[]{:S(2)}) copy-start(f32[8,256]{1,0:T(8,128)} %param.25) | copy-start | bytes 24580
  36.2 170.6 %all-gather.5.cloned.1.call-start = ((), (), s32[]{:S(2)}) async-start(), calls=%async_computation | async-start | bytes 3276800 | tf_op jit(solution)/shard_map/all_gather | solution.py:130
  95.4 4.5 %copy-start.6 = (bf16[128,5120]{0,1:T(8,128)(2,1)S(1)}, bf16[128,5120]{0,1:T(8,128)(2,1)}, u32[]{:S(2)}) copy-start(bf16[128,5120]{0,1:T(8,128)(2,1)} %copy.32) | copy-start | bytes 3932164
  164.8 3.4 %copy-start.1 = (bf16[256,5376]{1,0:T(8,128)(2,1)S(1)}, bf16[256,5376]{1,0:T(8,128)(2,1)}, u32[]{:S(2)}) copy-start(bf16[256,5376]{1,0:T(8,128)(2,1)} %copy-done) | copy-start | bytes 8257540
  168.1 5.3 %copy-start.10 = (f32[5120]{0:T(1024)S(1)}, f32[5120]{0:T(1024)}, u32[]{:S(2)}) copy-start(f32[5120]{0:T(1024)} %param.23) | copy-start | bytes 61444
  209.1 41.3 %copy-start.13 = (f32[8,256]{1,0:T(8,128)}, f32[8,256]{1,0:T(8,128)S(1)}, u32[]{:S(2)}) copy-start(f32[8,256]{1,0:T(8,128)S(1)} %get-tuple-element.82) | copy-start | bytes 24580
Sparse Core Ops, SparseCore 0:
  36.3 114.0 all-gather.6
  152.0 54.7 all-gather.4
where the time goes:
time: 258 us; the launch traced here: 257 us
  blocking collectives  96.3 us (37%)
  waiting for transfers between devices  77.4 us (30%)
  matrix products  30.7 us (12%)
  other arithmetic  18.5 us (7%)
  local copies, waits for them, and re-layouts  16.6 us (6%)
  between operations  15 us (6%)
    all_gather x1, waiting for transfers between devices, carried_in(): gathered = jax.tree.map(lambda a: lax.all_gather(a, axis), part)  46.5 us
    all_gather x1, blocking collectives, per_device(): lax.all_gather(prior_draw, ('dp', 'seq'), axis=0, tiled=True)  41.6 us
    all_gather x1, blocking collectives, per_device(): lax.all_gather(codes_local, ('dp', 'seq'), axis=0, tiled=True)  39.9 us
    all_gather x1, waiting for transfers between devices, per_device(): lax.all_gather(code_weight, 'dp', axis=0, tiled=True)  30.2 us
    unnamed x1, blocking collectives  14.7 us
    dot_general x2, matrix products, per_device(): jnp.einsum('tn,hpn->thp', read_block, start, precision=lax.Precision.HIGH...  10.6 us
    dot_general x2, matrix products, block_terms(): jnp.einsum('hts,shp->thp', mixing, values, preferred_element_type=jnp.flo...  8.53 us
    dot_general x2, matrix products, block_terms(): jnp.einsum('hsn,shp->hpn', weighted, values, preferred_element_type=jnp.f...  7.91 us
  transfers between devices with their start and end apart: 3, of which 2 were waited for; matrix products, arithmetic and copies ran while one was open for 14% of the time, Pallas kernels for 0%

commit v1 on v0

v1 whole, which is shorter than its diff:
```python
import functools

import jax
import jax.numpy as jnp
from jax import lax
from jax.experimental import pallas as pl
from jax.experimental.pallas import tpu as pltpu
from jax.sharding import PartitionSpec as P

SPAN = 128
SEG = 32
LANES = 128
CHUNK = 512
F32 = jnp.float32
BF16 = jnp.bfloat16
HIGH = lax.Precision.HIGHEST
MESH = pl.DeviceIdType.MESH
NT = (((1,), (1,)), ((), ()))


def silu(v):
    half = 0.5 * v
    return half + half * jnp.tanh(half)


def dot(a, b):
    return jnp.dot(a, b, preferred_element_type=F32)


def spread(rows, shift, unit):
    turned = pltpu.roll(rows, shift, 1)
    upper = turned.astype(BF16)
    lower = (turned - upper.astype(F32)).astype(BF16)
    return dot(jnp.concatenate([upper, lower], axis=1), unit)


def mixer_kernel(
    n_seq,
    head_dim,
    x_ref,
    gate_ref,
    write_ref,
    read_ref,
    steps_ref,
    logs_ref,
    taps_ref,
    bias_ref,
    skip_ref,
    gain_ref,
    mixed_ref,
    pooled_ref,
    rim_x,
    rim_w,
    rim_r,
    pad,
    values,
    total,
    inner_state,
    own_state,
    came,
    leaving,
    cum,
    cum_t,
    tail_t,
    grow_t,
    decays,
    unit,
    scores,
    write_t,
    reads,
    squares,
    scale,
    rim_send,
    rim_recv,
    send_sem,
    recv_sem,
):
    length, width = x_ref.shape
    heads = steps_ref.shape[0]
    taps = taps_ref.shape[0]
    chunks = width // CHUNK
    per_chunk = CHUNK // head_dim
    blocks = length // SPAN
    place = lax.axis_index("seq")
    has_left = place > 0
    has_right = place < n_seq - 1
    left = {"seq": jnp.maximum(place - 1, 0)}
    right = {"seq": jnp.minimum(place + 1, n_seq - 1)}

    barrier = pltpu.get_barrier_semaphore()

    @pl.when(has_left)
    def _():
        pl.semaphore_signal(barrier, inc=1, device_id=left, device_id_type=MESH)

    @pl.when(has_right)
    def _():
        pl.semaphore_signal(barrier, inc=1, device_id=right, device_id_type=MESH)

    neighbours = jnp.minimum(place, 1) + jnp.minimum(n_seq - 1 - place, 1)
    pl.semaphore_wait(barrier, neighbours)

    def rims():
        return [
            pltpu.make_async_remote_copy(
                src_ref=source.at[pl.ds(length - 16, 16)],
                dst_ref=target,
                send_sem=rim_send.at[k],
                recv_sem=rim_recv.at[k],
                device_id=right,
                device_id_type=MESH,
            )
            for k, (source, target) in enumerate(
                ((x_ref, rim_x), (write_ref, rim_w), (read_ref, rim_r))
            )
        ]

    def passing(j):
        return pltpu.make_async_remote_copy(
            src_ref=leaving.at[j],
            dst_ref=came.at[j],
            send_sem=send_sem.at[j],
            recv_sem=recv_sem.at[j],
            device_id=right,
            device_id_type=MESH,
        )

    @pl.when(has_right)
    def _():
        for copy in rims():
            copy.start()

    row = lax.broadcasted_iota(jnp.int32, (SPAN, SPAN), 0)
    col = lax.broadcasted_iota(jnp.int32, (SPAN, SPAN), 1)
    below = (row >= col).astype(F32)
    same = (row == col).astype(F32)
    cum[...] = jnp.zeros_like(cum)
    decays[...] = jnp.zeros_like(decays)
    pad_heads = jnp.zeros((LANES - heads, SPAN), F32)
    for b in range(blocks):
        span = pl.ds(b * SPAN, SPAN)
        logs = jnp.concatenate([logs_ref[:, span], pad_heads], axis=0)
        steps = jnp.concatenate([steps_ref[:, span], pad_heads], axis=0)
        cum[:, span] = lax.dot_general(logs, below, NT, precision=HIGH, preferred_element_type=F32)
        by_time = lax.dot_general(below, logs, NT, precision=HIGH, preferred_element_type=F32)
        steps_t = lax.dot_general(same, steps, NT, precision=HIGH, preferred_element_type=F32)
        cum_t[span, :] = by_time
        grow_t[span, :] = jnp.exp(by_time)
        tail_t[span, :] = jnp.exp(jnp.minimum(by_time[SPAN - 1 :, :] - by_time, 0.0)) * steps_t
        decays[b : b + 1, :] = jnp.exp(by_time[SPAN - 1 :, :])
    decays[blocks : blocks + 1, 0:heads] = skip_ref[...]
    k = lax.broadcasted_iota(jnp.int32, (2 * LANES, CHUNK), 0)
    c = lax.broadcasted_iota(jnp.int32, (2 * LANES, CHUNK), 1)
    unit[...] = jnp.where(k % LANES == c // head_dim, 1.0, 0.0).astype(BF16)
    squares[...] = jnp.zeros_like(squares)

    @pl.when(has_left)
    def _():
        for copy in rims():
            copy.wait_recv()

    @pl.when(jnp.logical_not(has_left))
    def _():
        rim_x[...] = jnp.zeros_like(rim_x)
        rim_w[...] = jnp.zeros_like(rim_w)
        rim_r[...] = jnp.zeros_like(rim_r)
        came[...] = jnp.zeros_like(came)

    def convolved(rim, body, columns, size):
        pad[0:8, 0:size] = rim.astype(F32)[8:16]
        pad[8 : 8 + length, 0:size] = body.astype(F32)
        result = bias_ref[:, columns] + taps_ref[taps - 1 : taps, columns] * body.astype(F32)
        for tap in range(taps - 1):
            shifted = pad[pl.ds(8 - (taps - 1) + tap, length), 0:size]
            result = result + taps_ref[tap : tap + 1, columns] * shifted
        return silu(result)

    state_dim = write_ref.shape[1]
    writes = convolved(rim_w[...], write_ref[...], pl.ds(width, state_dim), state_dim)
    reads[...] = convolved(
        rim_r[...], read_ref[...], pl.ds(width + state_dim, state_dim), state_dim
    ).astype(BF16)
    for b in range(blocks):
        span = pl.ds(b * SPAN, SPAN)
        flipped = writes[b * SPAN : (b + 1) * SPAN].T.astype(BF16)
        write_t[b] = flipped
        scores[b] = jnp.where(row >= col, dot(reads[span, :], flipped), 0.0)

    def turn(i):
        return lax.rem(LANES - per_chunk * i, LANES)

    def columns_of(i):
        return pl.ds(pl.multiple_of(i * CHUNK, CHUNK), CHUNK)

    def local_state(i):
        columns = columns_of(i)
        active = convolved(rim_x[:, columns], x_ref[:, columns], columns, CHUNK).astype(BF16)
        values[:, columns] = active
        shift = turn(i)
        scaled = (active.astype(F32) * spread(tail_t[...], shift, unit[...])).astype(BF16)
        decay = spread(decays[...], shift, unit[...])
        state = dot(write_t[0], scaled[0:SPAN])
        for b in range(1, blocks):
            inner_state[b - 1, :, columns] = state
            state = decay[b : b + 1] * state + dot(write_t[b], scaled[b * SPAN : (b + 1) * SPAN])
        own_state[i] = state

    def hand_on(j):
        @pl.when(has_left)
        def _():
            passing(j).wait_recv()

        @pl.when(has_right)
        def _():
            decay = spread(decays[...], turn(j), unit[...])
            whole = decay[0:1]
            for b in range(1, blocks):
                whole = whole * decay[b : b + 1]
            leaving[j] = (whole * came[j].astype(F32) + own_state[j]).astype(BF16)
            passing(j).start()

    def inner(i):
        columns_at = i * CHUNK
        turned = pltpu.roll(cum_t[...], turn(i), 1)
        rows = pl.ds(pl.multiple_of(i * per_chunk, per_chunk), per_chunk)
        logs = cum[rows, :]
        steps = steps_ref[rows, :]
        pair = LANES // head_dim
        lane = lax.broadcasted_iota(jnp.int32, (SPAN, LANES), 1) // head_dim
        for g in range(per_chunk // pair):
            columns = pl.ds(pl.multiple_of(columns_at + g * LANES, LANES), LANES)
            for b in range(blocks):
                lo, hi = b * SPAN, (b + 1) * SPAN
                both = values[lo:hi, columns]
                mix, parts = [], []
                for q in range(pair):
                    h = g * pair + q
                    gap = turned[lo:hi, h : h + 1] - logs[h : h + 1, lo:hi]
                    m = scores[b] * jnp.exp(jnp.minimum(gap, 0.0)) * steps[h : h + 1, lo:hi]
                    mix.append(m.astype(BF16))
                    parts.append(jnp.where(lane == q, both, jnp.zeros_like(both)))
                total[lo:hi, columns] = dot(
                    jnp.concatenate(mix, axis=1), jnp.concatenate(parts, axis=0)
                )

    lag = jnp.minimum(2 * place, chunks)

    def first_half(t, _):
        local_state(t)

        @pl.when(t >= lag)
        def _():
            hand_on(t - lag)

        return 0

    def second_half(t, _):
        inner(t)

        @pl.when(t + chunks - lag < chunks)
        def _():
            hand_on(t + chunks - lag)

        return 0

    lax.fori_loop(0, chunks, first_half, 0)
    lax.fori_loop(0, chunks, second_half, 0)

    def finish(j, _):
        columns = columns_of(j)
        shift = turn(j)
        grow = spread(grow_t[...], shift, unit[...])
        decay = spread(decays[...], shift, unit[...])
        carry = came[j]
        wide = carry.astype(F32)
        skip = decay[blocks : blocks + 1]
        ahead = None
        for b in range(blocks):
            lo, hi = b * SPAN, (b + 1) * SPAN
            if b:
                ahead = decay[b - 1 : b] if ahead is None else ahead * decay[b - 1 : b]
                carry = (inner_state[b - 1, :, columns] + ahead * wide).astype(BF16)
            outer = grow[lo:hi] * dot(reads[lo:hi, :], carry)
            out = total[lo:hi, columns] + outer + skip * values[lo:hi, columns].astype(F32)
            gated = out * silu(gate_ref[lo:hi, columns].astype(F32))
            total[lo:hi, columns] = gated
            power = gated * gated
            part = power[:, 0:LANES]
            for g in range(1, CHUNK // LANES):
                part = part + power[:, g * LANES : (g + 1) * LANES]
            squares[lo:hi, :] += part
        return 0

    lax.fori_loop(0, chunks, finish, 0)
    mean = jnp.sum(squares[...], axis=1, keepdims=True) * (1.0 / width)
    scale[...] = jnp.broadcast_to(lax.rsqrt(mean + 1e-05), scale.shape)
    segments = length // SEG
    seg_row = lax.broadcasted_iota(jnp.int32, (segments, length), 0)
    seg_col = lax.broadcasted_iota(jnp.int32, (segments, length), 1) // SEG
    pool = jnp.where(seg_row == seg_col, 1.0 / SEG, 0.0).astype(BF16)

    def norm(j, _):
        columns = columns_of(j)
        normed = (total[:, columns] * scale[:, 0:1] * gain_ref[:, columns]).astype(BF16)
        mixed_ref[:, columns] = normed
        pooled_ref[:, columns] = dot(pool, normed).astype(BF16).astype(F32)
        return 0

    lax.fori_loop(0, chunks, norm, 0)

    @pl.when(has_right)
    def _():
        for copy in rims():
            copy.wait_send()

        def sent(j, _):
            passing(j).wait_send()
            return 0

        lax.fori_loop(0, chunks, sent, 0)


def code_kernel(
    n_dp,
    n_seq,
    pooled_ref,
    weight_ref,
    prior_ref,
    codes_ref,
    kernel_ref,
    blocks_in,
    part_out,
    part_in,
    all_codes,
    all_prior,
    block_send,
    block_recv,
    part_send,
    part_recv,
    code_sems,
    prior_sems,
):
    n_dev = n_dp * n_seq
    depth, code_dim = weight_ref.shape
    rows = pooled_ref.shape[0]
    group = lax.axis_index("dp")
    place = lax.axis_index("seq")
    me = group * n_seq + place

    def device(offset):
        other = lax.rem(me + offset, n_dev)
        return {"dp": other // n_seq, "seq": lax.rem(other, n_seq)}

    barrier = pltpu.get_barrier_semaphore()

    def greet(offset, _):
        pl.semaphore_signal(barrier, inc=1, device_id=device(offset), device_id_type=MESH)
        return 0

    lax.fori_loop(1, n_dev, greet, 0)
    pl.semaphore_wait(barrier, n_dev - 1)

    def block_copy(o):
        to = lax.rem(group + o, n_dp)
        return pltpu.make_async_remote_copy(
            src_ref=pooled_ref.at[:, pl.ds(pl.multiple_of(to * depth, LANES), depth)],
            dst_ref=blocks_in.at[n_dp - o],
            send_sem=block_send.at[o],
            recv_sem=block_recv.at[n_dp - o],
            device_id={"dp": to},
            device_id_type=MESH,
        )

    def part_copy(o):
        to = lax.rem(group + o, n_dp)
        return pltpu.make_async_remote_copy(
            src_ref=part_out.at[o],
            dst_ref=part_in.at[n_dp - o],
            send_sem=part_send.at[o],
            recv_sem=part_recv.at[n_dp - o],
            device_id={"dp": to},
            device_id_type=MESH,
        )

    def to_all(source, target, sems):
        def one(offset, _):
            pltpu.make_async_remote_copy(
                src_ref=source,
                dst_ref=target.at[me],
                send_sem=sems.at[0],
                recv_sem=sems.at[1],
                device_id=device(offset),
                device_id_type=MESH,
            ).start()
            return 0

        lax.fori_loop(1, n_dev, one, 0)

    def all_done(target, sems, which):
        most = target.at[pl.ds(0, n_dev - 1)]
        pltpu.make_async_copy(most, most, sems.at[which]).wait()

    for o in range(1, n_dp):
        block_copy(o).start()
    to_all(prior_ref, all_prior, prior_sems)
    all_prior[me] = prior_ref[...]
    blocks_in[0] = pooled_ref[:, pl.ds(pl.multiple_of(group * depth, LANES), depth)]
    for o in range(1, n_dp):
        block_copy(o).wait_recv()
    gathered = blocks_in[...].reshape(n_dp * rows, depth).astype(BF16)
    part_out[...] = dot(gathered, weight_ref[...]).reshape(n_dp, rows, code_dim)
    for o in range(1, n_dp):
        part_copy(o).start()
    codes = part_out[0]
    for o in range(1, n_dp):
        part_copy(o).wait_recv()
    for o in range(1, n_dp):
        codes = codes + part_in[o]
    codes_ref[...] = codes
    to_all(codes_ref, all_codes, code_sems)
    all_codes[me] = codes
    row_sq = jnp.sum(codes * codes, axis=1, keepdims=True)
    ones = jnp.ones((rows, code_dim), F32)

    def against(columns):
        flat = columns.reshape(n_dev * rows, code_dim)
        cross = lax.dot_general(codes, flat, NT, precision=HIGH, preferred_element_type=F32)
        col_sq = lax.dot_general(ones, flat * flat, NT, precision=HIGH, preferred_element_type=F32)
        return 2.0 * code_dim / (2.0 * code_dim + (row_sq + col_sq - 2.0 * cross))

    all_done(all_prior, prior_sems, 1)
    kernel_ref[:, n_dev * rows :] = against(all_prior[...])
    all_done(all_codes, code_sems, 1)
    kernel_ref[:, : n_dev * rows] = against(all_codes[...])
    all_done(all_prior, prior_sems, 0)
    all_done(all_codes, code_sems, 0)
    for o in range(1, n_dp):
        block_copy(o).wait_send()
        part_copy(o).wait_send()


def per_device(
    n_dp,
    n_seq,
    inputs,
    gate_proj,
    write_proj,
    read_proj,
    step_size,
    log_forget,
    conv_weight,
    conv_bias,
    skip_gain,
    norm_gain,
    code_weight,
    prior_draw,
):
    length, width = inputs.shape[1:]
    state_dim = write_proj.shape[2]
    heads = step_size.shape[1]
    head_dim = width // heads
    chunks = width // CHUNK
    blocks = length // SPAN
    segments = length // SEG
    code_dim = code_weight.shape[1]
    n_dev = n_dp * n_seq
    vmem = pl.BlockSpec(memory_space=pltpu.VMEM)
    mixed, pooled = pl.pallas_call(
        functools.partial(mixer_kernel, n_seq, head_dim),
        out_shape=(
            jax.ShapeDtypeStruct((length, width), BF16),
            jax.ShapeDtypeStruct((segments, width), F32),
        ),
        in_specs=[vmem] * 10,
        out_specs=(vmem, vmem),
        scratch_shapes=[
            pltpu.VMEM((16, width), BF16),
            pltpu.VMEM((16, state_dim), BF16),
            pltpu.VMEM((16, state_dim), BF16),
            pltpu.VMEM((8 + length, CHUNK), F32),
            pltpu.VMEM((length, width), BF16),
            pltpu.VMEM((length, width), F32),
            pltpu.VMEM((blocks - 1, state_dim, width), F32),
            pltpu.VMEM((chunks, state_dim, CHUNK), F32),
            pltpu.VMEM((chunks, state_dim, CHUNK), BF16),
            pltpu.VMEM((chunks, state_dim, CHUNK), BF16),
            pltpu.VMEM((LANES, length), F32),
            pltpu.VMEM((length, LANES), F32),
            pltpu.VMEM((length, LANES), F32),
            pltpu.VMEM((length, LANES), F32),
            pltpu.VMEM((16, LANES), F32),
            pltpu.VMEM((2 * LANES, CHUNK), BF16),
            pltpu.VMEM((blocks, SPAN, SPAN), F32),
            pltpu.VMEM((blocks, state_dim, SPAN), BF16),
            pltpu.VMEM((length, state_dim), BF16),
            pltpu.VMEM((length, LANES), F32),
            pltpu.VMEM((length, LANES), F32),
            pltpu.SemaphoreType.DMA((3,)),
            pltpu.SemaphoreType.DMA((3,)),
            pltpu.SemaphoreType.DMA((chunks,)),
            pltpu.SemaphoreType.DMA((chunks,)),
        ],
        compiler_params=pltpu.CompilerParams(
            collective_id=0, has_side_effects=True, vmem_limit_bytes=48 * 1024 * 1024
        ),
        name="mixer",
    )(
        inputs[0],
        gate_proj[0],
        write_proj[0],
        read_proj[0],
        step_size[0],
        log_forget[0],
        conv_weight,
        conv_bias[None, :],
        skip_gain[None, :],
        norm_gain[None, :],
    )
    codes, kernel = pl.pallas_call(
        functools.partial(code_kernel, n_dp, n_seq),
        out_shape=(
            jax.ShapeDtypeStruct((segments, code_dim), F32),
            jax.ShapeDtypeStruct((segments, 2 * n_dev * segments), F32),
        ),
        in_specs=[vmem] * 3,
        out_specs=(vmem, vmem),
        scratch_shapes=[
            pltpu.VMEM((n_dp, segments, width // n_dp), F32),
            pltpu.VMEM((n_dp, segments, code_dim), F32),
            pltpu.VMEM((n_dp, segments, code_dim), F32),
            pltpu.VMEM((n_dev, segments, code_dim), F32),
            pltpu.VMEM((n_dev, segments, code_dim), F32),
            pltpu.SemaphoreType.DMA((n_dp,)),
            pltpu.SemaphoreType.DMA((n_dp,)),
            pltpu.SemaphoreType.DMA((n_dp,)),
            pltpu.SemaphoreType.DMA((n_dp,)),
            pltpu.SemaphoreType.DMA((2,)),
            pltpu.SemaphoreType.DMA((2,)),
        ],
        compiler_params=pltpu.CompilerParams(
            collective_id=1, has_side_effects=True, vmem_limit_bytes=48 * 1024 * 1024
        ),
        name="codes",
    )(pooled, code_weight, prior_draw)
    return (mixed[None], codes, kernel)


def solution(mesh):
    in_specs = (
        P("dp", "seq", None),
        P("dp", "seq", None),
        P("dp", "seq", None),
        P("dp", "seq", None),
        P("dp", None, "seq"),
        P("dp", None, "seq"),
        P(),
        P(),
        P(),
        P(),
        P("dp", None),
        P(("dp", "seq"), None),
    )
    out_specs = (P("dp", "seq", None), P(("dp", "seq"), None), P(("dp", "seq"), None))
    return jax.shard_map(
        functools.partial(per_device, mesh.shape["dp"], mesh.shape["seq"]),
        mesh=mesh,
        in_specs=in_specs,
        out_specs=out_specs,
        check_vma=False,
    )
```

time: 258 us -> 79.7 us (0.31)
  blocking collectives: 96.3 us -> 0 us
  waiting for transfers between devices: 77.4 us -> 0 us
  Pallas kernels: 0 us -> 67.6 us
  matrix products: 30.7 us -> 0 us
  other arithmetic: 18.5 us -> 0 us
  between operations: 15 us -> 0.68 us
  local copies, waits for them, and re-layouts: 16.6 us -> 10.9 us
    all_gather x2 -> x0, blocking collectives: 81.5 us -> none  [the longest x1 41.6 us: per_device(): lax.all_gather(prior_draw, ('dp', 'seq'), axis=0, tiled=True)]
    all_gather x2 -> x0, waiting for transfers between devices: 76.7 us -> none  [the longest x1 46.5 us: carried_in(): gathered = jax.tree.map(lambda a: lax.all_gather(a, axis), part)]
    pallas_call x0 -> x2, Pallas kernels: none -> 67.6 us  [the longest x1 39.9 us: per_device(): pl.pallas_call(functools.partial(code_kernel, n_dp, n_seq), out_shape=(ja...]
    dot_general x10 -> x0, matrix products: 30.7 us -> none  [the longest x2 10.6 us: per_device(): jnp.einsum('tn,hpn->thp', read_block, start, precision=lax.Precision.HIGH...]
    unnamed x1 -> x0, blocking collectives: 14.7 us -> none
    unnamed x40 -> x23, local copies, waits for them, and re-layouts: 2.38 us -> 10.2 us
    slice x6 -> x0, local copies, waits for them, and re-layouts: 7.09 us -> none  [the longest x3 6.83 us: per_device(): values[lower:upper]]
    concatenate x3 -> x0, local copies, waits for them, and re-layouts: 6.61 us -> none  [the longest x2 6.59 us: per_device(): ssd_out = jnp.concatenate(outputs, axis=0)]
  transfers between devices with their start and end apart: 3 -> 0, of which waited for: 2 -> 0; matrix products, arithmetic and copies ran while one was open for 14% -> 0% of each run, Pallas kernels for 0% -> 0%
where the time goes in v1:
time: 79.7 us; the launch traced here: 79.2 us
  Pallas kernels  67.6 us (85%)
  local copies, waits for them, and re-layouts  10.9 us (14%)
    pallas_call x1, Pallas kernels, per_device(): pl.pallas_call(functools.partial(code_kernel, n_dp, n_seq), out_shape=(ja...  39.9 us
    pallas_call x1, Pallas kernels, per_device(): pl.pallas_call(functools.partial(mixer_kernel, n_seq, head_dim), out_shap...  27.7 us
    unnamed x23, local copies, waits for them, and re-layouts  10.2 us

profile of v1, /device:TPU:0, one launch (start us, length us, event | category | flops | bytes accessed | tf_op | source)
XLA Modules:
  0.0 79.2 jit_solution(980069974075293435)
XLA Ops:
  0.6 0.8 broadcast_in_dim.12.bias_ref
  1.4 0.0 copy-start
  1.4 1.7 %copy-done = bf16[1,256,5120]{2,1,0:T(8,128)(2,1)S(1)} copy-done((bf16[1,256,5120]{2,1,0:T(8,128)(2,1)S(1)}, bf16[1,256,5120]{2,1,0:T(8,128)(2,1)}, u32[]{:S(2)}) %copy-start) | copy-done | bytes 2621464
  3.1 0.0 copy-start.2
  3.1 0.9 %copy-done.2 = f32[4,5376]{1,0:T(4,128)S(1)} copy-done((f32[4,5376]{1,0:T(4,128)S(1)}, f32[4,5376]{1,0:T(4,128)}, u32[]{:S(2)}) %copy-start.2) | copy-done | bytes 86040
  4.0 0.0 copy-start.3
  4.0 0.9 %copy-done.3 = f32[1,80,256]{2,1,0:T(8,128)S(1)} copy-done((f32[1,80,256]{2,1,0:T(8,128)S(1)}, f32[1,80,256]{2,1,0:T(8,128)}, u32[]{:S(2)}) %copy-start.3) | copy-done | bytes 81944
  4.9 0.0 copy-start.4
  4.9 0.9 %copy-done.4 = f32[1,80,256]{2,1,0:T(8,128)S(1)} copy-done((f32[1,80,256]{2,1,0:T(8,128)S(1)}, f32[1,80,256]{2,1,0:T(8,128)}, u32[]{:S(2)}) %copy-start.4) | copy-done | bytes 81944
  5.8 0.0 copy-start.5
  5.8 0.8 %copy-done.5 = bf16[1,256,128]{2,1,0:T(8,128)(2,1)S(1)} copy-done((bf16[1,256,128]{2,1,0:T(8,128)(2,1)S(1)}, bf16[1,256,128]{2,1,0:T(8,128)(2,1)}, u32[]{:S(2)}) %copy-start.5) | copy-done | bytes 65560
  6.6 0.0 copy-start.6
  6.6 0.8 %copy-done.6 = bf16[1,256,128]{2,1,0:T(8,128)(2,1)S(1)} copy-done((bf16[1,256,128]{2,1,0:T(8,128)(2,1)S(1)}, bf16[1,256,128]{2,1,0:T(8,128)(2,1)}, u32[]{:S(2)}) %copy-start.6) | copy-done | bytes 65560
  7.5 0.0 copy-start.7
  7.5 0.7 copy-done.7
  8.2 0.0 copy-start.9
  8.2 0.7 copy-done.9
  8.9 0.0 copy-start.1
  8.9 0.0 copy-start.8
  8.9 27.7 %mixer.1 = (bf16[256,5120]{1,0:T(8,128)(2,1)S(1)}, f32[8,5120]{1,0:T(8,128)S(1)}) custom-call(bf16[256,5120]{1,0:T(8,128)(2,1)S(1)} %bitcast.9, bf16[256,5120]{1,0:T(8,128)(2,1)} %bitcast.17, bf16[256,128]{1,0:T(8,128)(2,1)S(1)} %bitcast.13, bf16[256,128]{1,0:T(8,128)(2,1)S(1)} %bitcast.14, f32[80,256]{1,0:T(8,128)S(1)} %bitcast.11, f32[80,256]{1,0:T(8,128)S(1)} %bitcast.12, ...), custom_call_target="tpu_custom_call" | custom-call | tf_op jit(solution)/shard_map/mixer/pallas_call | solution.py:468
  36.5 0.0 copy-done.1
  36.5 0.0 copy-done.8
  36.5 39.9 %codes.1 = (f32[8,256]{1,0:T(8,128)S(1)}, f32[8,512]{1,0:T(8,128)S(1)}) custom-call(f32[8,5120]{1,0:T(8,128)S(1)} %get-tuple-element.8.pooled_ref, bf16[1280,256]{1,0:T(8,128)(2,1)S(1)} %copy-done.1, f32[8,256]{1,0:T(8,128)S(1)} %copy-done.8), custom_call_target="tpu_custom_call" | custom-call | tf_op jit(solution)/shard_map/codes/pallas_call | solution.py:519
  76.5 1.5 %copy.18 = bf16[1,256,5120]{2,1,0:T(8,128)(2,1)} copy(bf16[1,256,5120]{2,1,0:T(8,128)(2,1)S(1)} %bitcast.10) | data formatting | bytes 5242880
  78.0 0.6 copy.19
  78.6 0.6 copy.20
Async XLA Ops:
  1.4 1.7 %copy-start = (bf16[1,256,5120]{2,1,0:T(8,128)(2,1)S(1)}, bf16[1,256,5120]{2,1,0:T(8,128)(2,1)}, u32[]{:S(2)}) copy-start(bf16[1,256,5120]{2,1,0:T(8,128)(2,1)} %param.12) | copy-start | bytes 7864324
  3.1 0.9 %copy-start.2 = (f32[4,5376]{1,0:T(4,128)S(1)}, f32[4,5376]{1,0:T(4,128)}, u32[]{:S(2)}) copy-start(f32[4,5376]{1,0:T(4,128)} %taps_ref.1) | copy-start | bytes 258052
  4.0 0.9 %copy-start.3 = (f32[1,80,256]{2,1,0:T(8,128)S(1)}, f32[1,80,256]{2,1,0:T(8,128)}, u32[]{:S(2)}) copy-start(f32[1,80,256]{2,1,0:T(8,128)} %param.16) | copy-start | bytes 245764
  4.9 0.9 %copy-start.4 = (f32[1,80,256]{2,1,0:T(8,128)S(1)}, f32[1,80,256]{2,1,0:T(8,128)}, u32[]{:S(2)}) copy-start(f32[1,80,256]{2,1,0:T(8,128)} %param.17) | copy-start | bytes 245764
  5.8 0.8 %copy-start.5 = (bf16[1,256,128]{2,1,0:T(8,128)(2,1)S(1)}, bf16[1,256,128]{2,1,0:T(8,128)(2,1)}, u32[]{:S(2)}) copy-start(bf16[1,256,128]{2,1,0:T(8,128)(2,1)} %param.14) | copy-start | bytes 196612
  6.6 0.8 %copy-start.6 = (bf16[1,256,128]{2,1,0:T(8,128)(2,1)S(1)}, bf16[1,256,128]{2,1,0:T(8,128)(2,1)}, u32[]{:S(2)}) copy-start(bf16[1,256,128]{2,1,0:T(8,128)(2,1)} %param.15) | copy-start | bytes 196612
  7.5 0.7 copy-start.7
  8.2 0.7 copy-start.9
  8.9 27.7 %copy-start.1 = (bf16[1280,256]{1,0:T(8,128)(2,1)S(1)}, bf16[1280,256]{1,0:T(8,128)(2,1)}, u32[]{:S(2)}) copy-start(bf16[1280,256]{1,0:T(8,128)(2,1)} %weight_ref.1) | copy-start | bytes 1966084
  8.9 27.7 %copy-start.8 = (f32[8,256]{1,0:T(8,128)S(1)}, f32[8,256]{1,0:T(8,128)}, u32[]{:S(2)}) copy-start(f32[8,256]{1,0:T(8,128)} %prior_ref.1) | copy-start | bytes 24580

commit v2 on v1

--- a/solution.py
+++ b/solution.py
@@ -37,6 +37,18 @@
 def mixer_kernel(
     n_seq,
     head_dim,
+    x_hbm,
+    gate_hbm,
+    write_hbm,
+    read_hbm,
+    steps_hbm,
+    logs_hbm,
+    taps_hbm,
+    bias_hbm,
+    skip_hbm,
+    gain_hbm,
+    mixed_hbm,
+    pooled_ref,
     x_ref,
     gate_ref,
     write_ref,
@@ -48,7 +60,6 @@
     skip_ref,
     gain_ref,
     mixed_ref,
-    pooled_ref,
     rim_x,
     rim_w,
     rim_r,
@@ -70,11 +81,32 @@
     reads,
     squares,
     scale,
+    load_sem,
+    store_sem,
     rim_send,
     rim_recv,
     send_sem,
     recv_sem,
 ):
+    loads = [
+        pltpu.make_async_copy(source, target, load_sem.at[k])
+        for k, (source, target) in enumerate(
+            (
+                (logs_hbm, logs_ref),
+                (steps_hbm, steps_ref),
+                (skip_hbm, skip_ref),
+                (write_hbm, write_ref),
+                (read_hbm, read_ref),
+                (taps_hbm, taps_ref),
+                (bias_hbm, bias_ref),
+                (x_hbm, x_ref),
+                (gate_hbm, gate_ref),
+                (gain_hbm, gain_ref),
+            )
+        )
+    ]
+    for load in loads:
+        load.start()
     length, width = x_ref.shape
     heads = steps_ref.shape[0]
     taps = taps_ref.shape[0]
@@ -84,8 +116,8 @@
     place = lax.axis_index("seq")
     has_left = place > 0
     has_right = place < n_seq - 1
+    right = {"seq": jnp.minimum(place + 1, n_seq - 1)}
     left = {"seq": jnp.maximum(place - 1, 0)}
-    right = {"seq": jnp.minimum(place + 1, n_seq - 1)}
 
     barrier = pltpu.get_barrier_semaphore()
 
@@ -111,7 +143,7 @@
                 device_id_type=MESH,
             )
             for k, (source, target) in enumerate(
-                ((x_ref, rim_x), (write_ref, rim_w), (read_ref, rim_r))
+                ((x_hbm, rim_x), (write_hbm, rim_w), (read_hbm, rim_r))
             )
         ]
 
@@ -129,6 +161,9 @@
     def _():
         for copy in rims():
             copy.start()
+
+    for load in loads[0:3]:
+        load.wait()
 
     row = lax.broadcasted_iota(jnp.int32, (SPAN, SPAN), 0)
     col = lax.broadcasted_iota(jnp.int32, (SPAN, SPAN), 1)
@@ -154,6 +189,9 @@
     unit[...] = jnp.where(k % LANES == c // head_dim, 1.0, 0.0).astype(BF16)
     squares[...] = jnp.zeros_like(squares)
 
+    for load in loads[3:8]:
+        load.wait()
+
     @pl.when(has_left)
     def _():
         for copy in rims():
@@ -243,7 +281,8 @@
                     jnp.concatenate(mix, axis=1), jnp.concatenate(parts, axis=0)
                 )
 
-    lag = jnp.minimum(2 * place, chunks)
+    late = chunks + 4 * (place // 2 - 1) + lax.rem(place, 2)
+    lag = jnp.minimum(jnp.where(place < 2, 2 * place, late), 2 * chunks)
 
     def first_half(t, _):
         local_state(t)
@@ -257,16 +296,25 @@
     def second_half(t, _):
         inner(t)
 
-        @pl.when(t + chunks - lag < chunks)
+        j = t + chunks - lag
+
+        @pl.when(jnp.logical_and(j >= 0, j < chunks))
         def _():
-            hand_on(t + chunks - lag)
+            hand_on(j)
 
         return 0
 
     lax.fori_loop(0, chunks, first_half, 0)
     lax.fori_loop(0, chunks, second_half, 0)
 
+    for load in loads[8:]:
+        load.wait()
+
     def finish(j, _):
+        @pl.when(j + lag >= 2 * chunks)
+        def _():
+            hand_on(j)
+
         columns = columns_of(j)
         shift = turn(j)
         grow = spread(grow_t[...], shift, unit[...])
@@ -307,6 +355,9 @@
         return 0
 
     lax.fori_loop(0, chunks, norm, 0)
+    stored = pltpu.make_async_copy(mixed_ref, mixed_hbm, store_sem)
+
+    stored.start()
 
     @pl.when(has_right)
     def _():
@@ -318,6 +369,8 @@
             return 0
 
         lax.fori_loop(0, chunks, sent, 0)
+
+    stored.wait()
 
 
 def code_kernel(
@@ -331,112 +384,129 @@
     blocks_in,
     part_out,
     part_in,
-    all_codes,
-    all_prior,
+    gathered,
+    mine,
+    landed,
+    prior_in,
     block_send,
     block_recv,
     part_send,
     part_recv,
-    code_sems,
-    prior_sems,
+    prior_send,
+    prior_recv,
+    code_send,
+    code_recv,
 ):
-    n_dev = n_dp * n_seq
+    place = lax.axis_index("seq")
+    group = lax.axis_index("dp")
+
+    def along_dp(o):
+        return {"dp": lax.rem(group + o, n_dp)}
+
+    def along_seq(o):
+        return {"seq": lax.rem(place + o, n_seq)}
+
+    barrier = pltpu.get_barrier_semaphore()
+    for o in range(1, n_seq):
+        pl.semaphore_signal(barrier, inc=1, device_id=along_seq(o), device_id_type=MESH)
+    for o in range(1, n_dp):
+        pl.semaphore_signal(barrier, inc=1, device_id=along_dp(o), device_id_type=MESH)
+    pl.semaphore_wait(barrier, n_seq + n_dp - 2)
+
     depth, code_dim = weight_ref.shape
     rows = pooled_ref.shape[0]
-    group = lax.axis_index("dp")
-    place = lax.axis_index("seq")
-    me = group * n_seq + place
-
-    def device(offset):
-        other = lax.rem(me + offset, n_dev)
-        return {"dp": other // n_seq, "seq": lax.rem(other, n_seq)}
-
-    barrier = pltpu.get_barrier_semaphore()
-
-    def greet(offset, _):
-        pl.semaphore_signal(barrier, inc=1, device_id=device(offset), device_id_type=MESH)
-        return 0
-
-    lax.fori_loop(1, n_dev, greet, 0)
-    pl.semaphore_wait(barrier, n_dev - 1)
 
     def block_copy(o):
-        to = lax.rem(group + o, n_dp)
+        start = pl.multiple_of(lax.rem(group + o, n_dp) * depth, LANES)
         return pltpu.make_async_remote_copy(
-            src_ref=pooled_ref.at[:, pl.ds(pl.multiple_of(to * depth, LANES), depth)],
+            src_ref=pooled_ref.at[:, pl.ds(start, depth)],
             dst_ref=blocks_in.at[n_dp - o],
             send_sem=block_send.at[o],
             recv_sem=block_recv.at[n_dp - o],
-            device_id={"dp": to},
+            device_id=along_dp(o),
             device_id_type=MESH,
         )
 
     def part_copy(o):
-        to = lax.rem(group + o, n_dp)
         return pltpu.make_async_remote_copy(
-            src_ref=part_out.at[o],
+            src_ref=part_out,
             dst_ref=part_in.at[n_dp - o],
             send_sem=part_send.at[o],
             recv_sem=part_recv.at[n_dp - o],
-            device_id={"dp": to},
+            device_id=along_dp(o),
             device_id_type=MESH,
         )
 
-    def to_all(source, target, sems):
-        def one(offset, _):
-            pltpu.make_async_remote_copy(
-                src_ref=source,
-                dst_ref=target.at[me],
-                send_sem=sems.at[0],
-                recv_sem=sems.at[1],
-                device_id=device(offset),
-                device_id_type=MESH,
-            ).start()
-            return 0
-
-        lax.fori_loop(1, n_dev, one, 0)
-
-    def all_done(target, sems, which):
-        most = target.at[pl.ds(0, n_dev - 1)]
-        pltpu.make_async_copy(most, most, sems.at[which]).wait()
+    def column_copy(o):
+        return pltpu.make_async_remote_copy(
+            src_ref=mine,
+            dst_ref=landed.at[n_seq - o],
+            send_sem=code_send.at[o],
+            recv_sem=code_recv.at[n_seq - o],
+            device_id=along_seq(o),
+            device_id_type=MESH,
+        )
 
     for o in range(1, n_dp):
         block_copy(o).start()
-    to_all(prior_ref, all_prior, prior_sems)
-    all_prior[me] = prior_ref[...]
+
+    def prior_copy(o):
+        return pltpu.make_async_remote_copy(
+            src_ref=prior_ref,
+            dst_ref=prior_in.at[n_dp - o],
+            send_sem=prior_send.at[o],
+            recv_sem=prior_recv.at[n_dp - o],
+            device_id=along_dp(o),
+            device_id_type=MESH,
+        )
+
+    for o in range(1, n_dp):
+        prior_copy(o).start()
+    mine[n_dp + group] = prior_ref[...]
+    for o in range(1, n_dp):
+        prior_copy(o).wait_recv()
+    for o in range(1, n_dp):
+        mine[n_dp + lax.rem(group + o, n_dp)] = prior_in[o]
     blocks_in[0] = pooled_ref[:, pl.ds(pl.multiple_of(group * depth, LANES), depth)]
     for o in range(1, n_dp):
         block_copy(o).wait_recv()
-    gathered = blocks_in[...].reshape(n_dp * rows, depth).astype(BF16)
-    part_out[...] = dot(gathered, weight_ref[...]).reshape(n_dp, rows, code_dim)
+    pooled_rows = blocks_in[...].reshape(n_dp * rows, depth).astype(BF16)
+    part_out[...] = dot(pooled_rows, weight_ref[...]).reshape(n_dp, rows, code_dim)
     for o in range(1, n_dp):
         part_copy(o).start()
-    codes = part_out[0]
     for o in range(1, n_dp):
         part_copy(o).wait_recv()
-    for o in range(1, n_dp):
-        codes = codes + part_in[o]
+    summed = []
+    for r in range(n_dp):
+        rows_sum = part_out[r]
+        for o in range(1, n_dp):
+            rows_sum = rows_sum + part_in[o, (r - o) % n_dp]
+        summed.append(rows_sum)
+        mine[lax.rem(group + r, n_dp)] = rows_sum
+    for o in range(1, n_seq):
+        column_copy(o).start()
+    codes = summed[0]
     codes_ref[...] = codes
-    to_all(codes_ref, all_codes, code_sems)
-    all_codes[me] = codes
     row_sq = jnp.sum(codes * codes, axis=1, keepdims=True)
     ones = jnp.ones((rows, code_dim), F32)
-
-    def against(columns):
-        flat = columns.reshape(n_dev * rows, code_dim)
-        cross = lax.dot_general(codes, flat, NT, precision=HIGH, preferred_element_type=F32)
-        col_sq = lax.dot_general(ones, flat * flat, NT, precision=HIGH, preferred_element_type=F32)
-        return 2.0 * code_dim / (2.0 * code_dim + (row_sq + col_sq - 2.0 * cross))
-
-    all_done(all_prior, prior_sems, 1)
-    kernel_ref[:, n_dev * rows :] = against(all_prior[...])
-    all_done(all_codes, code_sems, 1)
-    kernel_ref[:, : n_dev * rows] = against(all_codes[...])
-    all_done(all_prior, prior_sems, 0)
-    all_done(all_codes, code_sems, 0)
-    for o in range(1, n_dp):
+    for o in range(1, n_seq):
+        column_copy(o).wait_recv()
+    gathered[place] = mine[...]
+    for o in range(1, n_seq):
+        gathered[lax.rem(place + o, n_seq)] = landed[o]
+    flat = jnp.concatenate(
+        [gathered[q, k] for k in range(2 * n_dp) for q in range(n_seq)], axis=0
+    )
+    cross = lax.dot_general(codes, flat, NT, precision=HIGH, preferred_element_type=F32)
+    col_sq = lax.dot_general(ones, flat * flat, NT, precision=HIGH, preferred_element_type=F32)
+    kernel_ref[...] = 2.0 * code_dim / (2.0 * code_dim + (row_sq + col_sq - 2.0 * cross))
+
+    for o in range(1, n_dp):
+        prior_copy(o).wait_send()
         block_copy(o).wait_send()
         part_copy(o).wait_send()
+    for o in range(1, n_seq):
+        column_copy(o).wait_send()
 
 
 def per_device(
@@ -465,15 +535,27 @@
     code_dim = code_weight.shape[1]
     n_dev = n_dp * n_seq
     vmem = pl.BlockSpec(memory_space=pltpu.VMEM)
+    anywhere = pl.BlockSpec(memory_space=pl.ANY)
     mixed, pooled = pl.pallas_call(
         functools.partial(mixer_kernel, n_seq, head_dim),
         out_shape=(
             jax.ShapeDtypeStruct((length, width), BF16),
             jax.ShapeDtypeStruct((segments, width), F32),
         ),
-        in_specs=[vmem] * 10,
-        out_specs=(vmem, vmem),
+        in_specs=[anywhere] * 10,
+        out_specs=(anywhere, vmem),
         scratch_shapes=[
+            pltpu.VMEM((length, width), BF16),
+            pltpu.VMEM((length, width), BF16),
+            pltpu.VMEM((length, state_dim), BF16),
+            pltpu.VMEM((length, state_dim), BF16),
+            pltpu.VMEM((heads, length), F32),
+            pltpu.VMEM((heads, length), F32),
+            pltpu.VMEM(conv_weight.shape, F32),
+            pltpu.VMEM((1, conv_bias.shape[0]), F32),
+            pltpu.VMEM((1, heads), F32),
+            pltpu.VMEM((1, width), F32),
+            pltpu.VMEM((length, width), BF16),
             pltpu.VMEM((16, width), BF16),
             pltpu.VMEM((16, state_dim), BF16),
             pltpu.VMEM((16, state_dim), BF16),
@@ -495,13 +577,15 @@
             pltpu.VMEM((length, state_dim), BF16),
             pltpu.VMEM((length, LANES), F32),
             pltpu.VMEM((length, LANES), F32),
+            pltpu.SemaphoreType.DMA((11,)),
+            pltpu.SemaphoreType.DMA,
             pltpu.SemaphoreType.DMA((3,)),
             pltpu.SemaphoreType.DMA((3,)),
             pltpu.SemaphoreType.DMA((chunks,)),
             pltpu.SemaphoreType.DMA((chunks,)),
         ],
         compiler_params=pltpu.CompilerParams(
-            collective_id=0, has_side_effects=True, vmem_limit_bytes=48 * 1024 * 1024
+            collective_id=0, has_side_effects=True, vmem_limit_bytes=60 * 1024 * 1024
         ),
         name="mixer",
     )(
@@ -527,15 +611,19 @@
         scratch_shapes=[
             pltpu.VMEM((n_dp, segments, width // n_dp), F32),
             pltpu.VMEM((n_dp, segments, code_dim), F32),
+            pltpu.VMEM((n_dp, n_dp, segments, code_dim), F32),
+            pltpu.VMEM((n_seq, 2 * n_dp, segments, code_dim), F32),
+            pltpu.VMEM((2 * n_dp, segments, code_dim), F32),
+            pltpu.VMEM((n_seq, 2 * n_dp, segments, code_dim), F32),
             pltpu.VMEM((n_dp, segments, code_dim), F32),
-            pltpu.VMEM((n_dev, segments, code_dim), F32),
-            pltpu.VMEM((n_dev, segments, code_dim), F32),
             pltpu.SemaphoreType.DMA((n_dp,)),
             pltpu.SemaphoreType.DMA((n_dp,)),
             pltpu.SemaphoreType.DMA((n_dp,)),
             pltpu.SemaphoreType.DMA((n_dp,)),
-            pltpu.SemaphoreType.DMA((2,)),
-            pltpu.SemaphoreType.DMA((2,)),
+            pltpu.SemaphoreType.DMA((n_dp,)),
+            pltpu.SemaphoreType.DMA((n_dp,)),
+            pltpu.SemaphoreType.DMA((n_seq,)),
+            pltpu.SemaphoreType.DMA((n_seq,)),
         ],
         compiler_params=pltpu.CompilerParams(
             collective_id=1, has_side_effects=True, vmem_limit_bytes=48 * 1024 * 1024

time: 79.7 us -> 75.3 us (0.945)
  local copies, waits for them, and re-layouts: 10.9 us -> 6.88 us
    unnamed x23 -> x9, local copies, waits for them, and re-layouts: 10.2 us -> 5.52 us
    pallas_call x1, Pallas kernels: 39.9 us -> 38.1 us  [per_device(): pl.pallas_call(functools.partial(code_kernel, n_dp, n_seq), out_shape=(ja...]
    pallas_call x1, Pallas kernels: 27.7 us -> 29 us  [per_device(): pl.pallas_call(functools.partial(mixer_kernel, n_seq, head_dim), out_shap...]
where the time goes in v2:
time: 75.3 us; the launch traced here: 74.7 us
  Pallas kernels  67.1 us (89%)
  local copies, waits for them, and re-layouts  6.88 us (9%)
    pallas_call x1, Pallas kernels, per_device(): pl.pallas_call(functools.partial(code_kernel, n_dp, n_seq), out_shape=(ja...  38.1 us
    pallas_call x1, Pallas kernels, per_device(): pl.pallas_call(functools.partial(mixer_kernel, n_seq, head_dim), out_shap...  29 us
    unnamed x9, local copies, waits for them, and re-layouts  5.52 us

profile of v2, /device:TPU:0, one launch (start us, length us, event | category | flops | bytes accessed | tf_op | source)
XLA Modules:
  0.0 74.7 jit_solution(10566501977570586526)
XLA Ops:
  0.6 1.4 %broadcast_in_dim.12.bias_hbm = f32[1,5376]{1,0:T(1,128)} reshape(f32[5376]{0:T(1024)} %param.19) | data formatting | bytes 43008 | tf_op jit(solution)/shard_map/broadcast_in_dim | solution.py:599
  2.0 0.0 copy-start
  2.0 0.0 copy-start.2
  2.0 29.0 %mixer.1 = (bf16[256,5120]{1,0:T(8,128)(2,1)}, f32[8,5120]{1,0:T(8,128)}) custom-call(bf16[256,5120]{1,0:T(8,128)(2,1)} %bitcast.9, bf16[256,5120]{1,0:T(8,128)(2,1)} %bitcast.10, bf16[256,128]{1,0:T(8,128)(2,1)} %bitcast.14, bf16[256,128]{1,0:T(8,128)(2,1)} %bitcast.15, f32[80,256]{1,0:T(8,128)} %bitcast.12, f32[80,256]{1,0:T(8,128)} %bitcast.13, ...), custom_call_target="tpu_custom_call" | custom-call | tf_op jit(solution)/shard_map/mixer/pallas_call | solution.py:539
  31.0 0.0 copy-done
  31.0 0.0 copy-done.2
  31.1 0.0 copy-start.1
  31.1 0.9 %copy-done.1 = f32[8,5120]{1,0:T(8,128)S(1)} copy-done((f32[8,5120]{1,0:T(8,128)S(1)}, f32[8,5120]{1,0:T(8,128)}, u32[]{:S(2)}) %copy-start.1) | copy-done | bytes 163864
  32.0 38.1 %codes.1 = (f32[8,256]{1,0:T(8,128)S(1)}, f32[8,512]{1,0:T(8,128)S(1)}) custom-call(f32[8,5120]{1,0:T(8,128)S(1)} %copy-done.1, bf16[1280,256]{1,0:T(8,128)(2,1)S(1)} %copy-done, f32[8,256]{1,0:T(8,128)S(1)} %copy-done.2), custom_call_target="tpu_custom_call" | custom-call | tf_op jit(solution)/shard_map/codes/pallas_call | solution.py:603
  70.1 3.4 %copy.18 = bf16[1,256,5120]{2,1,0:T(8,128)(2,1)} copy(bf16[1,256,5120]{2,1,0:T(8,128)(2,1)} %bitcast.11) | data formatting | bytes 5242880
  73.5 0.6 copy.19
  74.1 0.6 copy.20
Async XLA Ops:
  2.0 29.1 %copy-start = (bf16[1280,256]{1,0:T(8,128)(2,1)S(1)}, bf16[1280,256]{1,0:T(8,128)(2,1)}, u32[]{:S(2)}) copy-start(bf16[1280,256]{1,0:T(8,128)(2,1)} %weight_ref.1) | copy-start | bytes 1966084
  2.0 29.1 %copy-start.2 = (f32[8,256]{1,0:T(8,128)S(1)}, f32[8,256]{1,0:T(8,128)}, u32[]{:S(2)}) copy-start(f32[8,256]{1,0:T(8,128)} %prior_ref.1) | copy-start | bytes 24580
  31.1 0.9 %copy-start.1 = (f32[8,5120]{1,0:T(8,128)S(1)}, f32[8,5120]{1,0:T(8,128)}, u32[]{:S(2)}) copy-start(f32[8,5120]{1,0:T(8,128)} %get-tuple-element.8.pooled_ref) | copy-start | bytes 491524

commit v3 on v2

--- a/solution.py
+++ b/solution.py
@@ -281,8 +281,7 @@
                     jnp.concatenate(mix, axis=1), jnp.concatenate(parts, axis=0)
                 )
 
-    late = chunks + 4 * (place // 2 - 1) + lax.rem(place, 2)
-    lag = jnp.minimum(jnp.where(place < 2, 2 * place, late), 2 * chunks)
+    lag = jnp.minimum(2 * place, chunks)
 
     def first_half(t, _):
         local_state(t)

time: 75.3 us -> 74 us (0.983)
  Pallas kernels: 67.1 us -> 65.7 us
    pallas_call x1, Pallas kernels: 38.1 us -> 36.7 us  [per_device(): pl.pallas_call(functools.partial(code_kernel, n_dp, n_seq), out_shape=(ja...]
where the time goes in v3:
time: 74 us; the launch traced here: 73.3 us
  Pallas kernels  65.7 us (89%)
  local copies, waits for them, and re-layouts  6.88 us (9%)
    pallas_call x1, Pallas kernels, per_device(): pl.pallas_call(functools.partial(code_kernel, n_dp, n_seq), out_shape=(ja...  36.7 us
    pallas_call x1, Pallas kernels, per_device(): pl.pallas_call(functools.partial(mixer_kernel, n_seq, head_dim), out_shap...  29 us
    unnamed x9, local copies, waits for them, and re-layouts  5.52 us

profile of v3, /device:TPU:0, one launch (start us, length us, event | category | flops | bytes accessed | tf_op | source)
XLA Modules:
  0.0 73.3 jit_solution(4202651661030283943)
XLA Ops:
  0.6 1.4 %broadcast_in_dim.12.bias_hbm = f32[1,5376]{1,0:T(1,128)} reshape(f32[5376]{0:T(1024)} %param.19) | data formatting | bytes 43008 | tf_op jit(solution)/shard_map/broadcast_in_dim | solution.py:598
  2.0 0.0 copy-start
  2.0 0.0 copy-start.2
  2.0 29.0 %mixer.1 = (bf16[256,5120]{1,0:T(8,128)(2,1)}, f32[8,5120]{1,0:T(8,128)}) custom-call(bf16[256,5120]{1,0:T(8,128)(2,1)} %bitcast.9, bf16[256,5120]{1,0:T(8,128)(2,1)} %bitcast.10, bf16[256,128]{1,0:T(8,128)(2,1)} %bitcast.14, bf16[256,128]{1,0:T(8,128)(2,1)} %bitcast.15, f32[80,256]{1,0:T(8,128)} %bitcast.12, f32[80,256]{1,0:T(8,128)} %bitcast.13, ...), custom_call_target="tpu_custom_call" | custom-call | tf_op jit(solution)/shard_map/mixer/pallas_call | solution.py:538
  31.0 0.0 copy-done
  31.0 0.0 copy-done.2
  31.1 0.0 copy-start.1
  31.1 0.9 %copy-done.1 = f32[8,5120]{1,0:T(8,128)S(1)} copy-done((f32[8,5120]{1,0:T(8,128)S(1)}, f32[8,5120]{1,0:T(8,128)}, u32[]{:S(2)}) %copy-start.1) | copy-done | bytes 163864
  32.0 36.7 %codes.1 = (f32[8,256]{1,0:T(8,128)S(1)}, f32[8,512]{1,0:T(8,128)S(1)}) custom-call(f32[8,5120]{1,0:T(8,128)S(1)} %copy-done.1, bf16[1280,256]{1,0:T(8,128)(2,1)S(1)} %copy-done, f32[8,256]{1,0:T(8,128)S(1)} %copy-done.2), custom_call_target="tpu_custom_call" | custom-call | tf_op jit(solution)/shard_map/codes/pallas_call | solution.py:602
  68.7 3.4 %copy.18 = bf16[1,256,5120]{2,1,0:T(8,128)(2,1)} copy(bf16[1,256,5120]{2,1,0:T(8,128)(2,1)} %bitcast.11) | data formatting | bytes 5242880
  72.1 0.6 copy.19
  72.7 0.6 copy.20
Async XLA Ops:
  2.0 29.1 %copy-start = (bf16[1280,256]{1,0:T(8,128)(2,1)S(1)}, bf16[1280,256]{1,0:T(8,128)(2,1)}, u32[]{:S(2)}) copy-start(bf16[1280,256]{1,0:T(8,128)(2,1)} %weight_ref.1) | copy-start | bytes 1966084
  2.0 29.1 %copy-start.2 = (f32[8,256]{1,0:T(8,128)S(1)}, f32[8,256]{1,0:T(8,128)}, u32[]{:S(2)}) copy-start(f32[8,256]{1,0:T(8,128)} %prior_ref.1) | copy-start | bytes 24580
  31.1 0.9 %copy-start.1 = (f32[8,5120]{1,0:T(8,128)S(1)}, f32[8,5120]{1,0:T(8,128)}, u32[]{:S(2)}) copy-start(f32[8,5120]{1,0:T(8,128)} %get-tuple-element.8.pooled_ref) | copy-start | bytes 491524
